TPU v7x, 256 devices: a whole 4x4x8 slice. The times are simulated.
256 devices in a mesh: emx: 8 (over y, x_hi), emy: 16 (over z, core), grp: 2 (over x_lo).
Axes of the slice: x: 4 (x_hi: 2, x_lo: 2; x = x_hi * 2 + x_lo), y: 4, z: 8, core: 2. Of those that a mesh axis runs over, the one named last changes fastest.
Arguments:
- efield: float32 [3, 12, 256, 4096], P(None, None, 'emx', ('emy', 'grp')), may hold values from -6 to 6
- hfield: float32 [3, 12, 256, 4096], P(None, None, 'emx', ('emy', 'grp')), may hold values from -6 to 6
- magnet: float32 [3, 8, 256, 4096], P(None, None, ('emx', 'emy', 'grp')), may hold values from -6 to 6
- material: int32 [256, 4096], P('emx', ('emy', 'grp')), may hold values from 0 to 3
- drive: float32 [256, 4096], P('emx', ('emy', 'grp')), may hold values from -6 to 6
Outputs:
- efield_new: float32 [3, 12, 256, 4096], P(None, None, 'emx', ('emy', 'grp'))
- hfield_new: float32 [3, 12, 256, 4096], P(None, None, 'emx', ('emy', 'grp'))
- magnet_new: float32 [3, 8, 256, 4096], P(None, None, ('emx', 'emy', 'grp'))
All inputs are finite; a program needn't handle non-finite values.
Results may differ from a plain program's by a relative error of at most 0.00002.
Values sent between devices are 32-bit elements; how exact they have to be, the bound alone decides.
A program may use at most 64 MiB of HBM per device.

v0:
```python
import functools

import jax
import jax.numpy as jnp
from jax import lax
from jax.experimental import pallas as pl
from jax.experimental.pallas import tpu as pltpu
from jax.sharding import PartitionSpec as P

FZ = 8
W = 8

step_dt = 0.5
film_eps = 15.0
exch_coef = 0.25
gyro_coef = 0.3
damp_coef = 0.1

MESH = pl.DeviceIdType.MESH
LANES = 128
CUT = 5
HALF = FZ // 2
PITCH = 16
TILE = 8


def grade(index, count):
    edge = jnp.minimum(index, count - 1 - index)
    depth = jnp.maximum(W - edge, 0).astype(jnp.float32) / W
    return 0.4 * depth * depth


def spread_order(count):
    half = count // 2
    order = [half]
    for step in range(1, half):
        order += [half + step, half - step]
    return order


def step_kernel(
    sizes,
    e_in, h_in, m_in, mat_in, drv_in,
    e, h, m,
    mat, drv,
    chunk_a, chunk_b, got_a, got_b,
    hx_send, hx_got, hy_send, hy_got,
    ex_send, ex_got, ey_send, ey_got,
    back, back_got,
    load_sem, send_sem, halo_sem, wave_sem, edge_sem, back_sem,
):
    nz, rows, count_x, group, emy, grp = sizes
    tiles = rows // TILE
    film = 3 * FZ
    a = lax.axis_index("emx")
    b = lax.axis_index("emy") * grp + lax.axis_index("grp")

    def peer(index):
        return {"emx": a, "emy": index // grp, "grp": lax.rem(index, grp)}

    a_next, a_prev = lax.rem(a + 1, count_x), lax.rem(a + count_x - 1, count_x)
    b_next, b_prev = lax.rem(b + 1, group), lax.rem(b + group - 1, group)
    to_a_next, to_a_prev = {"emx": a_next}, {"emx": a_prev}
    order = spread_order(group)

    def layers(ref, lo, hi, comp):
        first = (comp * FZ + lo) * rows
        return ref.at[pl.ds(first, (hi - lo) * rows)]

    m_loads = [
        [
            pltpu.make_async_copy(
                layers(m_in, lo, hi, comp), layers(m, lo, hi, comp), load_sem.at[4 + 3 * wave + comp]
            )
            for comp in range(3)
        ]
        for wave, (lo, hi) in enumerate(((0, CUT), (CUT, FZ)))
    ]
    loads = [
        pltpu.make_async_copy(src, dst, load_sem.at[i])
        for i, (src, dst) in enumerate(((h_in, h), (e_in, e), (mat_in, mat), (drv_in, drv)))
    ]
    for load in m_loads[0] + m_loads[1] + loads:
        load.start()

    barrier = pltpu.get_barrier_semaphore()
    for k in order:
        pl.semaphore_signal(
            barrier, inc=1, device_id=peer(lax.rem(b + k, group)), device_id_type=MESH
        )
    for device in (to_a_next, to_a_prev):
        pl.semaphore_signal(barrier, inc=1, device_id=device, device_id_type=MESH)

    lane = lax.broadcasted_iota(jnp.int32, (TILE, LANES), 1)
    wide = lax.broadcasted_iota(jnp.int32, (rows, LANES), 1)
    deep = lax.broadcasted_iota(jnp.int32, (rows, LANES), 0)

    def column(tile, at):
        return jnp.broadcast_to(tile[:, at : at + 1], (TILE, LANES))

    def wait_all(copies):
        for copy in copies:
            copy.wait()

    def place(z):
        return (chunk_a, z) if z < CUT else (chunk_b, z - CUT)

    def fill(lo, hi, lasts, firsts):
        for t in range(tiles):
            for comp in range(3):
                for z in range(lo, hi):
                    q = comp * FZ + z
                    v = m[pl.ds(q * rows + t * TILE, TILE), :]
                    ref, layer = place(z)
                    ref[pl.ds(t * TILE * PITCH + layer * 3 + comp, TILE, stride=PITCH), :] = v
                    lasts[t] = jnp.where(lane == q, column(v, LANES - 1), lasts[t])
                    firsts[t] = jnp.where(lane == film + q, column(v, 0), firsts[t])

    blank = jnp.zeros((TILE, LANES), jnp.float32)
    lasts, firsts = [blank] * tiles, [blank] * tiles
    wait_all(m_loads[0])
    fill(0, CUT, lasts, firsts)
    wait_all(m_loads[1])
    fill(CUT, FZ, lasts, firsts)
    last = jnp.concatenate(lasts, axis=0)
    first = jnp.concatenate(firsts, axis=0)
    last = jnp.where(deep == 0, 0.0, pltpu.roll(last, 1, 0))
    first = jnp.where(deep == rows - 1, 0.0, pltpu.roll(first, rows - 1, 0))
    edges = jnp.where(wide < film, last, first)
    for t in range(tiles):
        chunk_a[pl.ds(t * TILE * PITCH + 3 * CUT, TILE, stride=PITCH), :] = edges[
            t * TILE : (t + 1) * TILE
        ]

    def field(ref, comp, z):
        return ref[pl.ds((comp * nz + z) * rows, rows), :]

    def tile_of(ref, comp, z, t):
        return ref[pl.ds((comp * nz + z) * rows + t * TILE, TILE), :]

    def pack(ref, comps, at):
        packed = jnp.zeros((TILE, LANES), jnp.float32)
        for n, comp in enumerate(comps):
            for z in range(nz):
                for t in range(tiles):
                    v = tile_of(ref, comp, z, t)
                    packed = jnp.where(
                        lane == (n * nz + z) * tiles + t, column(v, at), packed
                    )
        return packed

    def unpack(packed, n, z):
        first = (n * nz + z) * tiles
        return jnp.concatenate([column(packed, first + t) for t in range(tiles)], axis=0)

    loads[0].wait()
    for n, comp in enumerate((1, 2)):
        hx_send[pl.ds(n * nz, nz), :] = h[
            pl.ds(comp * nz * rows + rows - 1, nz, stride=rows), :
        ]
    hy_send[...] = pack(h, (0, 2), LANES - 1)

    pl.semaphore_wait(barrier, group + 1)

    def halo(src, dst, which, device):
        copy = pltpu.make_async_remote_copy(
            src_ref=src,
            dst_ref=dst,
            send_sem=halo_sem.at[0, which],
            recv_sem=halo_sem.at[1, which],
            device_id=device,
            device_id_type=MESH,
        )
        copy.start()
        return copy

    def block(ref, index, size):
        return ref.at[pl.ds(pl.multiple_of(index * PITCH, PITCH), size)]

    hx = halo(hx_send, hx_got, 0, to_a_next)
    hy = halo(hy_send, hy_got, 1, peer(b_next))
    kind = (b + group - 2) // (group - 1) + b // (group - 1)
    waves = ((chunk_a, got_a, 3 * CUT + 1), (chunk_b, got_b, 3 * (FZ - CUT)))

    def send_wave(wave, part):
        src, dst, size = waves[wave]
        for k in part:
            j = lax.rem(b + k, group)
            pltpu.make_async_remote_copy(
                src_ref=block(src, j, size),
                dst_ref=block(dst, b + 1, size),
                send_sem=send_sem.at[wave],
                recv_sem=wave_sem.at[wave, kind],
                device_id=peer(j),
                device_id_type=MESH,
            ).start()

    for wave, (src, dst, size) in enumerate(waves):
        pltpu.make_async_copy(
            block(src, b, size), block(dst, b + 1, size), wave_sem.at[wave, kind]
        ).start()
    send_wave(0, order)

    for load in loads[1:]:
        load.wait()
    index_x = a * rows + deep
    index_y = b * LANES + wide
    sigma = grade(index_x, count_x * rows) + grade(index_y, group * LANES)
    decay = (1.0 - sigma) / (1.0 + sigma)
    hstep = step_dt / (1.0 + sigma)
    film_step = step_dt / (film_eps * (1.0 + sigma))
    material = mat[...]
    eps = jnp.where(
        material == 0, 1.0, jnp.where(material == 1, 2.2, jnp.where(material == 2, 4.4, 9.8))
    ).astype(jnp.float32)
    upper_step = step_dt / (eps * (1.0 + sigma))

    hx.wait()
    hy.wait()
    left = jnp.where(b == 0, 0.0, hy_got[...])

    def below_x(v, n, z):
        edge = jnp.where(a == 0, 0.0, hx_got[pl.ds(n * nz + z, 1), :])
        return jnp.where(deep == 0, edge, pltpu.roll(v, 1, 0))

    def below_y(v, n, z):
        return jnp.where(wide == 0, unpack(left, n, z), pltpu.roll(v, 1, 1))

    under = None
    for z in range(nz):
        hx_z, hy_z, hz_z = (field(h, comp, z) for comp in range(3))
        back_zy = hz_z - below_y(hz_z, 1, z)
        back_zx = hz_z - below_x(hz_z, 1, z)
        back_yx = hy_z - below_x(hy_z, 0, z)
        back_xy = hx_z - below_y(hx_z, 0, z)
        back_yz = hy_z if under is None else hy_z - under[1]
        back_xz = hx_z if under is None else hx_z - under[0]
        comp_x = back_zy - back_yz
        if z == nz - 1:
            comp_x = comp_x - drv[...]
        comp_y = back_xz - back_zx
        comp_z = back_yx - back_xy
        estep = film_step if z < FZ else upper_step
        for comp, value in enumerate((comp_x, comp_y, comp_z)):
            e[pl.ds((comp * nz + z) * rows, rows), :] = decay * field(e, comp, z) + estep * value
        under = (hx_z, hy_z)

    for n, comp in enumerate((1, 2)):
        ex_send[pl.ds(n * nz, nz), :] = e[pl.ds(comp * nz * rows, nz, stride=rows), :]
    ey_send[...] = pack(e, (0, 2), 0)
    ex = halo(ex_send, ex_got, 2, to_a_prev)
    ey = halo(ey_send, ey_got, 3, peer(b_prev))
    send_wave(1, order)

    def wait_wave(wave, which, count):
        _, dst, size = waves[wave]
        landed = dst.at[pl.ds(0, count * size)]
        pltpu.make_async_copy(landed, landed, wave_sem.at[wave, which]).wait()

    def edge(wave, src, dst, which, device):
        _, ref, size = waves[wave]
        copy = pltpu.make_async_remote_copy(
            src_ref=block(ref, src, size),
            dst_ref=block(ref, dst, size),
            send_sem=edge_sem.at[0, wave, which],
            recv_sem=edge_sem.at[1, wave, which],
            device_id=device,
            device_id_type=MESH,
        )
        copy.start()
        return copy

    def pass_on(wave):
        wait_wave(wave, 0, 1)
        low = edge(wave, 1, rows + 1, 0, to_a_prev)
        wait_wave(wave, 2, 1)
        high = edge(wave, rows, 0, 1, to_a_next)
        return low, high

    passed = [pass_on(0), None]

    ex.wait()
    ey.wait()
    right = jnp.where(b == group - 1, 0.0, ey_got[...])

    def above_x(v, n, z):
        edge = jnp.where(a == count_x - 1, 0.0, ex_got[pl.ds(n * nz + z, 1), :])
        return jnp.where(deep == rows - 1, edge, pltpu.roll(v, rows - 1, 0))

    def above_y(v, n, z):
        return jnp.where(wide == LANES - 1, unpack(right, n, z), pltpu.roll(v, LANES - 1, 1))

    for z in range(nz):
        ex_z, ey_z, ez_z = (field(e, comp, z) for comp in range(3))
        fore_zy = above_y(ez_z, 1, z) - ez_z
        fore_zx = above_x(ez_z, 1, z) - ez_z
        fore_yx = above_x(ey_z, 0, z) - ey_z
        fore_xy = above_y(ex_z, 0, z) - ex_z
        fore_yz = (field(e, 1, z + 1) if z < nz - 1 else 0.0) - ey_z
        fore_xz = (field(e, 0, z + 1) if z < nz - 1 else 0.0) - ex_z
        curls = (fore_zy - fore_yz, fore_xz - fore_zx, fore_yx - fore_xy)
        for comp, value in enumerate(curls):
            h[pl.ds((comp * nz + z) * rows, rows), :] = decay * field(h, comp, z) - hstep * value

    def spin(first, count, stride, half):
        def take(ref, base, pitch):
            return ref[pl.ds(base, count, stride=pitch), :]

        sides = take(got_a, (first + 1) * PITCH + 3 * CUT, stride * PITCH)
        lane = lax.broadcasted_iota(jnp.int32, (count, LANES), 1)

        def column(tile, at):
            return jnp.broadcast_to(tile[:, at : at + 1], (count, LANES))

        def spins(comp, z, shift):
            ref, layer = (got_a, z) if z < CUT else (got_b, z - CUT)
            return take(ref, (first + 1 + shift) * PITCH + layer * 3 + comp, stride * PITCH)

        for layer in range(HALF):
            z = half * HALF + layer
            centre = [spins(comp, z, 0) for comp in range(3)]
            heff = []
            for comp in range(3):
                v = centre[comp]
                q = comp * FZ + z
                y_up = jnp.where(
                    lane == LANES - 1, column(sides, film + q), pltpu.roll(v, LANES - 1, 1)
                )
                y_down = jnp.where(lane == 0, column(sides, q), pltpu.roll(v, 1, 1))
                lap = spins(comp, z, 1) + spins(comp, z, -1) + y_up + y_down
                if z < FZ - 1:
                    lap = lap + spins(comp, z + 1, 0)
                if z > 0:
                    lap = lap + spins(comp, z - 1, 0)
                lap = lap - 6.0 * v
                value = take(h, (comp * nz + z) * rows + first, stride) + exch_coef * lap
                if comp == 2:
                    value = value + 1.0 + 0.5 * v
                heff.append(value)
            mx, my, mz = centre
            tx = my * heff[2] - mz * heff[1]
            ty = mz * heff[0] - mx * heff[2]
            tz = mx * heff[1] - my * heff[0]
            dx = -gyro_coef * (tx + damp_coef * (my * tz - mz * ty))
            dy = -gyro_coef * (ty + damp_coef * (mz * tx - mx * tz))
            dz = -gyro_coef * (tz + damp_coef * (mx * ty - my * tx))
            for comp, d in enumerate((dx, dy, dz)):
                at = pl.ds((comp * nz + z) * rows + first, count, stride=stride)
                h[at, :] = h[at, :] - d
            big_x, big_y = largest(mx, my, mz)
            u = jnp.where(big_x, dy, jnp.where(big_y, dz, dx))
            v = jnp.where(big_x, dz, jnp.where(big_y, dx, dy))
            at = (half * rows + first) * 2 * HALF + 2 * layer
            back[pl.ds(at, count, stride=stride * 2 * HALF), :] = u
            back[pl.ds(at + 1, count, stride=stride * 2 * HALF), :] = v

    def part(ref, half, index):
        first = (half * group + index) * 2 * HALF
        return ref.at[pl.ds(pl.multiple_of(first, 2 * HALF), 2 * HALF)]

    def send_back(indices, half):
        for i in indices:

            @pl.when(b != i)
            def _():
                pltpu.make_async_remote_copy(
                    src_ref=part(back, half, i),
                    dst_ref=part(back_got, half, b),
                    send_sem=send_sem.at[2 + half],
                    recv_sem=back_sem.at[half],
                    device_id={"emx": a, "emy": i // grp, "grp": i % grp},
                    device_id_type=MESH,
                ).start()

            @pl.when(b == i)
            def _():
                pltpu.make_async_copy(
                    part(back, half, i), part(back_got, half, b), back_sem.at[half]
                ).start()

    def inner(half):
        wait_wave(half, 1, rows - 2)
        for first in range(1, rows - 1, TILE):
            count = min(TILE, rows - 1 - first)
            spin(first, count, 1, half)
            send_back(range(first, first + count), half)

    def outer(half):
        for copy in passed[half]:
            copy.wait()
        ref = waves[half][1]

        @pl.when(a == 0)
        def _():
            ref[pl.ds(0, PITCH), :] = jnp.zeros((PITCH, LANES), jnp.float32)

        @pl.when(a == count_x - 1)
        def _():
            ref[pl.ds((rows + 1) * PITCH, PITCH), :] = jnp.zeros((PITCH, LANES), jnp.float32)

        spin(0, 2, rows - 1, half)
        send_back((0, rows - 1), half)

    inner(0)
    passed[1] = pass_on(1)
    outer(0)
    inner(1)
    outer(1)

    for half in range(2):
        landed = back_got.at[pl.ds(half * group * 2 * HALF, group * 2 * HALF)]
        pltpu.make_async_copy(landed, landed, back_sem.at[half]).wait()
        for t in range(tiles):
            for layer in range(HALF):
                z = half * HALF + layer
                places = [pl.ds((comp * FZ + z) * rows + t * TILE, TILE) for comp in range(3)]
                mx, my, mz = (m[at, :] for at in places)
                at = (half * group + t * TILE) * 2 * HALF + 2 * layer
                u = back_got[pl.ds(at, TILE, stride=2 * HALF), :]
                v = back_got[pl.ds(at + 1, TILE, stride=2 * HALF), :]
                big_x, big_y = largest(mx, my, mz)
                big = jnp.where(big_x, mx, jnp.where(big_y, my, mz))
                mu = jnp.where(big_x, my, jnp.where(big_y, mz, mx))
                mv = jnp.where(big_x, mz, jnp.where(big_y, mx, my))
                tiny = jnp.abs(big) < 1e-30
                scale = jnp.where(tiny, 0.0, 1.0 / jnp.where(tiny, 1.0, big))
                w = -((mu * scale) * u + (mv * scale) * v)
                m[places[0], :] = mx + jnp.where(big_x, w, jnp.where(big_y, v, u))
                m[places[1], :] = my + jnp.where(big_x, u, jnp.where(big_y, w, v))
                m[places[2], :] = mz + jnp.where(big_x, v, jnp.where(big_y, u, w))

    for sem, size in enumerate((3 * CUT + 1, 3 * (FZ - CUT), 2 * HALF, 2 * HALF)):
        sent = chunk_a.at[pl.ds(0, (group - 1) * size)]
        pltpu.make_async_copy(sent, sent, send_sem.at[sem]).wait()


def store_kernel(e, h, m, e_out, h_out, m_out, sem):
    pairs = ((e, e_out), (h, h_out), (m, m_out))
    copies = [pltpu.make_async_copy(src, dst, sem.at[i]) for i, (src, dst) in enumerate(pairs)]
    for copy in copies:
        copy.start()
    for copy in copies:
        copy.wait()


def largest(mx, my, mz):
    sx, sy, sz = jnp.abs(mx), jnp.abs(my), jnp.abs(mz)
    big_x = (sx >= sy) & (sx >= sz)
    big_y = sy >= sz
    return big_x, big_y


def shards(efield, hfield, magnet, material, drive):
    _, nz, rows, cols_y = efield.shape
    count_x = lax.axis_size("emx")
    emy, grp = lax.axis_size("emy"), lax.axis_size("grp")
    group = emy * grp
    assert cols_y == LANES and rows == group and magnet.shape[2] == 1
    film = 3 * FZ
    tiles = rows // TILE
    assert 2 * nz * tiles <= LANES and 2 * film <= LANES
    f32 = jnp.float32
    field_shape = (3 * nz * rows, LANES)
    spin_shape = (film * group, LANES)
    dma = pltpu.SemaphoreType.DMA
    any_spec = pl.BlockSpec(memory_space=pl.ANY)
    sizes = (nz, rows, count_x, group, emy, grp)
    vmem_spec = pl.BlockSpec(memory_space=pltpu.VMEM)
    operands = [
        pltpu.with_memory_space_constraint(operand, pltpu.HBM)
        for operand in (
            efield.reshape(field_shape),
            hfield.reshape(field_shape),
            magnet.reshape(spin_shape),
            material,
            drive,
        )
    ]
    held = pl.pallas_call(
        functools.partial(step_kernel, sizes),
        out_shape=(
            pltpu.VMEM(field_shape, f32),
            pltpu.VMEM(field_shape, f32),
            pltpu.VMEM(spin_shape, f32),
        ),
        in_specs=[any_spec] * 5,
        out_specs=[vmem_spec] * 3,
        scratch_shapes=[
            pltpu.VMEM((rows, LANES), jnp.int32),
            pltpu.VMEM((rows, LANES), f32),
            pltpu.VMEM((group * PITCH, LANES), f32),
            pltpu.VMEM((group * PITCH, LANES), f32),
            pltpu.VMEM(((rows + 2) * PITCH, LANES), f32),
            pltpu.VMEM(((rows + 2) * PITCH, LANES), f32),
            pltpu.VMEM((2 * nz, LANES), f32),
            pltpu.VMEM((2 * nz, LANES), f32),
            pltpu.VMEM((TILE, LANES), f32),
            pltpu.VMEM((TILE, LANES), f32),
            pltpu.VMEM((2 * nz, LANES), f32),
            pltpu.VMEM((2 * nz, LANES), f32),
            pltpu.VMEM((TILE, LANES), f32),
            pltpu.VMEM((TILE, LANES), f32),
            pltpu.VMEM((rows * 2 * FZ, LANES), f32),
            pltpu.VMEM((group * 2 * FZ, LANES), f32),
            dma((10,)),
            dma((4,)),
            dma((2, 4)),
            dma((2, 3)),
            dma((2, 2, 2)),
            dma((2,)),
        ],
        compiler_params=pltpu.CompilerParams(
            collective_id=0, has_side_effects=True, vmem_limit_bytes=32 * 1024 * 1024
        ),
    )(*operands)
    outs = pl.pallas_call(
        store_kernel,
        out_shape=(
            jax.ShapeDtypeStruct(field_shape, f32),
            jax.ShapeDtypeStruct(field_shape, f32),
            jax.ShapeDtypeStruct(spin_shape, f32),
        ),
        in_specs=[vmem_spec] * 3,
        out_specs=[any_spec] * 3,
        scratch_shapes=[dma((3,))],
    )(*(pltpu.with_memory_space_constraint(part, pltpu.VMEM) for part in held))
    return (
        outs[0].reshape(efield.shape),
        outs[1].reshape(hfield.shape),
        outs[2].reshape(magnet.shape),
    )


def solution(mesh):
    return jax.shard_map(
        shards,
        mesh=mesh,
        in_specs=(
            P(None, None, "emx", ("emy", "grp")),
            P(None, None, "emx", ("emy", "grp")),
            P(None, None, ("emx", "emy", "grp"), None),
            P("emx", ("emy", "grp")),
            P("emx", ("emy", "grp")),
        ),
        out_specs=(
            P(None, None, "emx", ("emy", "grp")),
            P(None, None, "emx", ("emy", "grp")),
            P(None, None, ("emx", "emy", "grp"), None),
        ),
        check_vma=False,
    )
```

profile of v0, /device:TPU:1, one launch (start us, length us, event | category | flops | bytes accessed | tf_op | source)
XLA Modules:
  0.0 32.1 jit_solution(10283042497998071275)
XLA Ops:
  0.6 30.3 %shard_map.76 = (f32[1152,128]{1,0:T(8,128)S(1)}, f32[1152,128]{1,0:T(8,128)S(1)}, f32[768,128]{1,0:T(8,128)S(1)}) custom-call(f32[1152,128]{1,0:T(8,128)} %bitcast.6, f32[1152,128]{1,0:T(8,128)} %bitcast.7, f32[768,128]{1,0:T(8,128)} %bitcast.8, s32[32,128]{1,0:T(8,128)} %mat_in.1, f32[32,128]{1,0:T(8,128)} %drv_in.1), custom_call_target="tpu_custom_call" | custom-call | tf_op jit(solution)/shard_map/pallas_call | solution.py:479
  30.9 1.2 %shard_map.77 = (f32[1152,128]{1,0:T(8,128)}, f32[1152,128]{1,0:T(8,128)}, f32[768,128]{1,0:T(8,128)}) custom-call(f32[1152,128]{1,0:T(8,128)S(1)} %get-tuple-element.9.e, f32[1152,128]{1,0:T(8,128)S(1)} %get-tuple-element.10.h, f32[768,128]{1,0:T(8,128)S(1)} %get-tuple-element.11.m), custom_call_target="tpu_custom_call" | custom-call | tf_op jit(solution)/shard_map/pallas_call | solution.py:516
where the time goes:
time: 32.2 us; the launch traced here: 32.1 us
  Pallas kernels  31.4 us (98%)
  between operations  0.64 us (2%)
    pallas_call x1, Pallas kernels, shards(): pl.pallas_call(functools.partial(step_kernel, sizes), out_shape=(pltpu.VM...  30.3 us
    pallas_call x1, Pallas kernels, shards(): pl.pallas_call(store_kernel, out_shape=(jax.ShapeDtypeStruct(field_shape,...  1.16 us

commit v1 on v0

--- a/solution.py
+++ b/solution.py
@@ -21,6 +21,8 @@
 CUT = 5
 HALF = FZ // 2
 PITCH = 16
+SEATS = 4
+MIDDLE = 25
 TILE = 8
 
 
@@ -30,12 +32,8 @@
     return 0.4 * depth * depth
 
 
-def spread_order(count):
-    half = count // 2
-    order = [half]
-    for step in range(1, half):
-        order += [half + step, half - step]
-    return order
+def far_first(count):
+    return sorted(range(1, count), key=lambda step: -min(step, count - step))
 
 
 def step_kernel(
@@ -47,7 +45,7 @@
     hx_send, hx_got, hy_send, hy_got,
     ex_send, ex_got, ey_send, ey_got,
     back, back_got,
-    load_sem, send_sem, halo_sem, wave_sem, edge_sem, back_sem,
+    load_sem, ready_sem, send_sem, halo_sem, wave_sem, edge_sem, back_sem,
 ):
     nz, rows, count_x, group, emy, grp = sizes
     tiles = rows // TILE
@@ -61,7 +59,17 @@
     a_next, a_prev = lax.rem(a + 1, count_x), lax.rem(a + count_x - 1, count_x)
     b_next, b_prev = lax.rem(b + 1, group), lax.rem(b + group - 1, group)
     to_a_next, to_a_prev = {"emx": a_next}, {"emx": a_prev}
-    order = spread_order(group)
+    has_next, has_prev = a < count_x - 1, a > 0
+    plane, seat = b // SEATS, lax.rem(b, SEATS)
+    far = far_first(group // SEATS)
+    same_seat = [(step, 0) for step in far]
+    mates = [(0, turn) for turn in range(1, SEATS)]
+    others = [(step, turn) for turn in range(1, SEATS) for step in far]
+
+    def member(offset):
+        step, turn = offset
+        planes = group // SEATS
+        return lax.rem(plane + step, planes) * SEATS + lax.rem(seat + turn, SEATS)
 
     def layers(ref, lo, hi, comp):
         first = (comp * FZ + lo) * rows
@@ -84,12 +92,20 @@
         load.start()
 
     barrier = pltpu.get_barrier_semaphore()
-    for k in order:
-        pl.semaphore_signal(
-            barrier, inc=1, device_id=peer(lax.rem(b + k, group)), device_id_type=MESH
-        )
-    for device in (to_a_next, to_a_prev):
+
+    def greet(device):
         pl.semaphore_signal(barrier, inc=1, device_id=device, device_id_type=MESH)
+
+    for offset in same_seat + mates:
+        greet(peer(member(offset)))
+
+    @pl.when(has_next)
+    def _():
+        greet(to_a_next)
+
+    @pl.when(has_prev)
+    def _():
+        greet(to_a_prev)
 
     lane = lax.broadcasted_iota(jnp.int32, (TILE, LANES), 1)
     wide = lax.broadcasted_iota(jnp.int32, (rows, LANES), 1)
@@ -160,10 +176,8 @@
         ]
     hy_send[...] = pack(h, (0, 2), LANES - 1)
 
-    pl.semaphore_wait(barrier, group + 1)
-
     def halo(src, dst, which, device):
-        copy = pltpu.make_async_remote_copy(
+        return pltpu.make_async_remote_copy(
             src_ref=src,
             dst_ref=dst,
             send_sem=halo_sem.at[0, which],
@@ -171,8 +185,20 @@
             device_id=device,
             device_id_type=MESH,
         )
-        copy.start()
-        return copy
+
+    def go(copy, sends):
+        @pl.when(sends)
+        def _():
+            copy.start()
+
+    def land(copy, sends, receives):
+        @pl.when(receives)
+        def _():
+            copy.wait_recv()
+
+        @pl.when(sends)
+        def _():
+            copy.wait_send()
 
     def block(ref, index, size):
         return ref.at[pl.ds(pl.multiple_of(index * PITCH, PITCH), size)]
@@ -184,8 +210,8 @@
 
     def send_wave(wave, part):
         src, dst, size = waves[wave]
-        for k in part:
-            j = lax.rem(b + k, group)
+        for offset in part:
+            j = member(offset)
             pltpu.make_async_remote_copy(
                 src_ref=block(src, j, size),
                 dst_ref=block(dst, b + 1, size),
@@ -199,7 +225,18 @@
         pltpu.make_async_copy(
             block(src, b, size), block(dst, b + 1, size), wave_sem.at[wave, kind]
         ).start()
-    send_wave(0, order)
+    pl.semaphore_wait(
+        barrier, len(same_seat + mates) + jnp.int32(has_next) + jnp.int32(has_prev)
+    )
+    for offset in mates:
+        pl.semaphore_signal(
+            ready_sem, inc=1, device_id=peer(member(offset)), device_id_type=MESH
+        )
+    send_wave(0, same_seat)
+    pl.semaphore_wait(ready_sem, len(mates))
+    go(hx, has_next)
+    hy.start()
+    send_wave(0, others + mates)
 
     for load in loads[1:]:
         load.wait()
@@ -215,12 +252,12 @@
     ).astype(jnp.float32)
     upper_step = step_dt / (eps * (1.0 + sigma))
 
-    hx.wait()
+    land(hx, has_next, has_prev)
     hy.wait()
     left = jnp.where(b == 0, 0.0, hy_got[...])
 
     def below_x(v, n, z):
-        edge = jnp.where(a == 0, 0.0, hx_got[pl.ds(n * nz + z, 1), :])
+        edge = jnp.where(has_prev, hx_got[pl.ds(n * nz + z, 1), :], 0.0)
         return jnp.where(deep == 0, edge, pltpu.roll(v, 1, 0))
 
     def below_y(v, n, z):
@@ -250,7 +287,9 @@
     ey_send[...] = pack(e, (0, 2), 0)
     ex = halo(ex_send, ex_got, 2, to_a_prev)
     ey = halo(ey_send, ey_got, 3, peer(b_prev))
-    send_wave(1, order)
+    go(ex, has_prev)
+    ey.start()
+    send_wave(1, same_seat + others + mates)
 
     def wait_wave(wave, which, count):
         _, dst, size = waves[wave]
@@ -259,7 +298,7 @@
 
     def edge(wave, src, dst, which, device):
         _, ref, size = waves[wave]
-        copy = pltpu.make_async_remote_copy(
+        return pltpu.make_async_remote_copy(
             src_ref=block(ref, src, size),
             dst_ref=block(ref, dst, size),
             send_sem=edge_sem.at[0, wave, which],
@@ -267,24 +306,24 @@
             device_id=device,
             device_id_type=MESH,
         )
-        copy.start()
-        return copy
 
     def pass_on(wave):
-        wait_wave(wave, 0, 1)
+        high = edge(wave, rows, 0, 1, to_a_next)
         low = edge(wave, 1, rows + 1, 0, to_a_prev)
         wait_wave(wave, 2, 1)
-        high = edge(wave, rows, 0, 1, to_a_next)
+        go(high, has_next)
+        wait_wave(wave, 0, 1)
+        go(low, has_prev)
         return low, high
 
     passed = [pass_on(0), None]
 
-    ex.wait()
+    land(ex, has_prev, has_next)
     ey.wait()
     right = jnp.where(b == group - 1, 0.0, ey_got[...])
 
     def above_x(v, n, z):
-        edge = jnp.where(a == count_x - 1, 0.0, ex_got[pl.ds(n * nz + z, 1), :])
+        edge = jnp.where(has_next, ex_got[pl.ds(n * nz + z, 1), :], 0.0)
         return jnp.where(deep == rows - 1, edge, pltpu.roll(v, rows - 1, 0))
 
     def above_y(v, n, z):
@@ -378,34 +417,41 @@
                     part(back, half, i), part(back_got, half, b), back_sem.at[half]
                 ).start()
 
-    def inner(half):
-        wait_wave(half, 1, rows - 2)
-        for first in range(1, rows - 1, TILE):
-            count = min(TILE, rows - 1 - first)
+    def inner(half, lo, hi):
+        for first in range(lo, hi, TILE):
+            count = min(TILE, hi - first)
             spin(first, count, 1, half)
             send_back(range(first, first + count), half)
 
-    def outer(half):
-        for copy in passed[half]:
-            copy.wait()
+    def outer(half, row):
+        low, high = passed[half]
         ref = waves[half][1]
-
-        @pl.when(a == 0)
+        if row == 0:
+            land(high, has_next, has_prev)
+            known, ghost = has_prev, 0
+        else:
+            land(low, has_prev, has_next)
+            known, ghost = has_next, rows + 1
+
+        @pl.when(jnp.logical_not(known))
         def _():
-            ref[pl.ds(0, PITCH), :] = jnp.zeros((PITCH, LANES), jnp.float32)
-
-        @pl.when(a == count_x - 1)
-        def _():
-            ref[pl.ds((rows + 1) * PITCH, PITCH), :] = jnp.zeros((PITCH, LANES), jnp.float32)
-
-        spin(0, 2, rows - 1, half)
-        send_back((0, rows - 1), half)
-
-    inner(0)
+            ref[pl.ds(ghost * PITCH, PITCH), :] = jnp.zeros((PITCH, LANES), jnp.float32)
+
+        spin(row, 1, 1, half)
+        send_back((row,), half)
+
+    middle = min(MIDDLE, rows - 1)
+    wait_wave(0, 1, rows - 2)
+    inner(0, 1, middle)
+    outer(0, 0)
+    inner(0, middle, rows - 1)
     passed[1] = pass_on(1)
-    outer(0)
-    inner(1)
-    outer(1)
+    outer(0, rows - 1)
+    wait_wave(1, 1, rows - 2)
+    inner(1, 1, middle)
+    outer(1, 0)
+    inner(1, middle, rows - 1)
+    outer(1, rows - 1)
 
     for half in range(2):
         landed = back_got.at[pl.ds(half * group * 2 * HALF, group * 2 * HALF)]
@@ -503,6 +549,7 @@
             pltpu.VMEM((rows * 2 * FZ, LANES), f32),
             pltpu.VMEM((group * 2 * FZ, LANES), f32),
             dma((10,)),
+            pltpu.SemaphoreType.REGULAR,
             dma((4,)),
             dma((2, 4)),
             dma((2, 3)),

time: 32.2 us -> 29.8 us (0.925)
  the two profiles are of different devices: /device:TPU:1 before, /device:TPU:24 now
where the time goes in v1:
time: 29.8 us; the launch traced here: 29.7 us
  Pallas kernels  29.1 us (98%)
  between operations  0.64 us (2%)
    pallas_call x1, Pallas kernels, shards(): pl.pallas_call(functools.partial(step_kernel, sizes), out_shape=(pltpu.VM...  27.9 us
    pallas_call x1, Pallas kernels, shards(): pl.pallas_call(store_kernel, out_shape=(jax.ShapeDtypeStruct(field_shape,...  1.16 us

profile of v1, /device:TPU:24, one launch (start us, length us, event | category | flops | bytes accessed | tf_op | source)
XLA Modules:
  0.0 29.7 jit_solution(10162160936014571029)
XLA Ops:
  0.6 27.9 %shard_map.76 = (f32[1152,128]{1,0:T(8,128)S(1)}, f32[1152,128]{1,0:T(8,128)S(1)}, f32[768,128]{1,0:T(8,128)S(1)}) custom-call(f32[1152,128]{1,0:T(8,128)} %bitcast.6, f32[1152,128]{1,0:T(8,128)} %bitcast.7, f32[768,128]{1,0:T(8,128)} %bitcast.8, s32[32,128]{1,0:T(8,128)} %mat_in.1, f32[32,128]{1,0:T(8,128)} %drv_in.1), custom_call_target="tpu_custom_call" | custom-call | tf_op jit(solution)/shard_map/pallas_call | solution.py:525
  28.6 1.2 %shard_map.77 = (f32[1152,128]{1,0:T(8,128)}, f32[1152,128]{1,0:T(8,128)}, f32[768,128]{1,0:T(8,128)}) custom-call(f32[1152,128]{1,0:T(8,128)S(1)} %get-tuple-element.9.e, f32[1152,128]{1,0:T(8,128)S(1)} %get-tuple-element.10.h, f32[768,128]{1,0:T(8,128)S(1)} %get-tuple-element.11.m), custom_call_target="tpu_custom_call" | custom-call | tf_op jit(solution)/shard_map/pallas_call | solution.py:563

commit v2 on v1

--- a/solution.py
+++ b/solution.py
@@ -22,7 +22,7 @@
 HALF = FZ // 2
 PITCH = 16
 SEATS = 4
-MIDDLE = 25
+CUTS = (9, 25, 9)
 TILE = 8
 
 
@@ -39,12 +39,12 @@
 def step_kernel(
     sizes,
     e_in, h_in, m_in, mat_in, drv_in,
-    e, h, m,
+    e, h, m, back_got,
     mat, drv,
     chunk_a, chunk_b, got_a, got_b,
     hx_send, hx_got, hy_send, hy_got,
     ex_send, ex_got, ey_send, ey_got,
-    back, back_got,
+    back,
     load_sem, ready_sem, send_sem, halo_sem, wave_sem, edge_sem, back_sem,
 ):
     nz, rows, count_x, group, emy, grp = sizes
@@ -237,6 +237,11 @@
     go(hx, has_next)
     hy.start()
     send_wave(0, others + mates)
+
+    @pl.when(b == rows - 1)
+    def _():
+        send_wave(1, same_seat + others + mates)
+
 
     for load in loads[1:]:
         load.wait()
@@ -289,7 +294,10 @@
     ey = halo(ey_send, ey_got, 3, peer(b_prev))
     go(ex, has_prev)
     ey.start()
-    send_wave(1, same_seat + others + mates)
+
+    @pl.when(b != rows - 1)
+    def _():
+        send_wave(1, same_seat + others + mates)
 
     def wait_wave(wave, which, count):
         _, dst, size = waves[wave]
@@ -307,16 +315,19 @@
             device_id_type=MESH,
         )
 
-    def pass_on(wave):
-        high = edge(wave, rows, 0, 1, to_a_next)
-        low = edge(wave, 1, rows + 1, 0, to_a_prev)
+    high = [edge(wave, rows, 0, 1, to_a_next) for wave in range(2)]
+    low = [edge(wave, 1, rows + 1, 0, to_a_prev) for wave in range(2)]
+
+    def pass_high(wave):
         wait_wave(wave, 2, 1)
-        go(high, has_next)
+        go(high[wave], has_next)
+
+    def pass_low(wave):
         wait_wave(wave, 0, 1)
-        go(low, has_prev)
-        return low, high
-
-    passed = [pass_on(0), None]
+        go(low[wave], has_prev)
+
+    pass_high(0)
+    pass_low(0)
 
     land(ex, has_prev, has_next)
     ey.wait()
@@ -424,13 +435,12 @@
             send_back(range(first, first + count), half)
 
     def outer(half, row):
-        low, high = passed[half]
         ref = waves[half][1]
         if row == 0:
-            land(high, has_next, has_prev)
+            land(high[half], has_next, has_prev)
             known, ghost = has_prev, 0
         else:
-            land(low, has_prev, has_next)
+            land(low[half], has_prev, has_next)
             known, ghost = has_next, rows + 1
 
         @pl.when(jnp.logical_not(known))
@@ -440,51 +450,71 @@
         spin(row, 1, 1, half)
         send_back((row,), half)
 
-    middle = min(MIDDLE, rows - 1)
+    cuts = [min(cut, rows - 1) for cut in CUTS]
     wait_wave(0, 1, rows - 2)
-    inner(0, 1, middle)
+    inner(0, 1, cuts[0])
+    pass_high(1)
+    inner(0, cuts[0], cuts[1])
     outer(0, 0)
-    inner(0, middle, rows - 1)
-    passed[1] = pass_on(1)
+    inner(0, cuts[1], rows - 1)
+    pass_low(1)
     outer(0, rows - 1)
     wait_wave(1, 1, rows - 2)
-    inner(1, 1, middle)
+    inner(1, 1, cuts[2])
     outer(1, 0)
-    inner(1, middle, rows - 1)
+    inner(1, cuts[2], rows - 1)
     outer(1, rows - 1)
 
     for half in range(2):
         landed = back_got.at[pl.ds(half * group * 2 * HALF, group * 2 * HALF)]
         pltpu.make_async_copy(landed, landed, back_sem.at[half]).wait()
-        for t in range(tiles):
-            for layer in range(HALF):
-                z = half * HALF + layer
-                places = [pl.ds((comp * FZ + z) * rows + t * TILE, TILE) for comp in range(3)]
-                mx, my, mz = (m[at, :] for at in places)
-                at = (half * group + t * TILE) * 2 * HALF + 2 * layer
-                u = back_got[pl.ds(at, TILE, stride=2 * HALF), :]
-                v = back_got[pl.ds(at + 1, TILE, stride=2 * HALF), :]
-                big_x, big_y = largest(mx, my, mz)
-                big = jnp.where(big_x, mx, jnp.where(big_y, my, mz))
-                mu = jnp.where(big_x, my, jnp.where(big_y, mz, mx))
-                mv = jnp.where(big_x, mz, jnp.where(big_y, mx, my))
-                tiny = jnp.abs(big) < 1e-30
-                scale = jnp.where(tiny, 0.0, 1.0 / jnp.where(tiny, 1.0, big))
-                w = -((mu * scale) * u + (mv * scale) * v)
-                m[places[0], :] = mx + jnp.where(big_x, w, jnp.where(big_y, v, u))
-                m[places[1], :] = my + jnp.where(big_x, u, jnp.where(big_y, w, v))
-                m[places[2], :] = mz + jnp.where(big_x, v, jnp.where(big_y, u, w))
+        if half == 0:
+            turn_magnet(m, back_got, group, half)
 
     for sem, size in enumerate((3 * CUT + 1, 3 * (FZ - CUT), 2 * HALF, 2 * HALF)):
         sent = chunk_a.at[pl.ds(0, (group - 1) * size)]
         pltpu.make_async_copy(sent, sent, send_sem.at[sem]).wait()
 
 
-def store_kernel(e, h, m, e_out, h_out, m_out, sem):
-    pairs = ((e, e_out), (h, h_out), (m, m_out))
-    copies = [pltpu.make_async_copy(src, dst, sem.at[i]) for i, (src, dst) in enumerate(pairs)]
+def turn_magnet(m, back_got, rows, half):
+    for t in range(rows // TILE):
+        for layer in range(HALF):
+            z = half * HALF + layer
+            places = [pl.ds((comp * FZ + z) * rows + t * TILE, TILE) for comp in range(3)]
+            mx, my, mz = (m[at, :] for at in places)
+            at = (half * rows + t * TILE) * 2 * HALF + 2 * layer
+            u = back_got[pl.ds(at, TILE, stride=2 * HALF), :]
+            v = back_got[pl.ds(at + 1, TILE, stride=2 * HALF), :]
+            big_x, big_y = largest(mx, my, mz)
+            big = jnp.where(big_x, mx, jnp.where(big_y, my, mz))
+            mu = jnp.where(big_x, my, jnp.where(big_y, mz, mx))
+            mv = jnp.where(big_x, mz, jnp.where(big_y, mx, my))
+            tiny = jnp.abs(big) < 1e-30
+            scale = jnp.where(tiny, 0.0, 1.0 / jnp.where(tiny, 1.0, big))
+            w = -((mu * scale) * u + (mv * scale) * v)
+            m[places[0], :] = mx + jnp.where(big_x, w, jnp.where(big_y, v, u))
+            m[places[1], :] = my + jnp.where(big_x, u, jnp.where(big_y, w, v))
+            m[places[2], :] = mz + jnp.where(big_x, v, jnp.where(big_y, u, w))
+
+
+def store_kernel(rows, e, h, m, back_got, e_out, h_out, m_out, part, sem):
+    size = HALF * rows
+    copies = [
+        pltpu.make_async_copy(src, dst, sem.at[i]) for i, (src, dst) in enumerate(((e, e_out), (h, h_out)))
+    ]
+    for comp in range(3):
+        at = pl.ds(comp * FZ * rows, size)
+        copies.append(pltpu.make_async_copy(m.at[at], m_out.at[at], sem.at[2 + comp]))
     for copy in copies:
         copy.start()
+    for comp in range(3):
+        part[pl.ds((comp * FZ + HALF) * rows, size), :] = m[pl.ds((comp * FZ + HALF) * rows, size), :]
+    turn_magnet(part, back_got, rows, 1)
+    for comp in range(3):
+        at = pl.ds((comp * FZ + HALF) * rows, size)
+        copy = pltpu.make_async_copy(part.at[at], m_out.at[at], sem.at[5 + comp])
+        copy.start()
+        copies.append(copy)
     for copy in copies:
         copy.wait()
 
@@ -528,9 +558,10 @@
             pltpu.VMEM(field_shape, f32),
             pltpu.VMEM(field_shape, f32),
             pltpu.VMEM(spin_shape, f32),
+            pltpu.VMEM((group * 2 * FZ, LANES), f32),
         ),
         in_specs=[any_spec] * 5,
-        out_specs=[vmem_spec] * 3,
+        out_specs=[vmem_spec] * 4,
         scratch_shapes=[
             pltpu.VMEM((rows, LANES), jnp.int32),
             pltpu.VMEM((rows, LANES), f32),
@@ -547,7 +578,6 @@
             pltpu.VMEM((TILE, LANES), f32),
             pltpu.VMEM((TILE, LANES), f32),
             pltpu.VMEM((rows * 2 * FZ, LANES), f32),
-            pltpu.VMEM((group * 2 * FZ, LANES), f32),
             dma((10,)),
             pltpu.SemaphoreType.REGULAR,
             dma((4,)),
@@ -561,15 +591,15 @@
         ),
     )(*operands)
     outs = pl.pallas_call(
-        store_kernel,
+        functools.partial(store_kernel, rows),
         out_shape=(
             jax.ShapeDtypeStruct(field_shape, f32),
             jax.ShapeDtypeStruct(field_shape, f32),
             jax.ShapeDtypeStruct(spin_shape, f32),
         ),
-        in_specs=[vmem_spec] * 3,
+        in_specs=[vmem_spec] * 4,
         out_specs=[any_spec] * 3,
-        scratch_shapes=[dma((3,))],
+        scratch_shapes=[pltpu.VMEM(spin_shape, f32), dma((8,))],
     )(*(pltpu.with_memory_space_constraint(part, pltpu.VMEM) for part in held))
     return (
         outs[0].reshape(efield.shape),

time: 29.8 us -> 28.8 us (0.966)
  Pallas kernels: 29.1 us -> 28 us
    pallas_call x1, Pallas kernels: 27.9 us -> 26.8 us  [shards(): pl.pallas_call(functools.partial(step_kernel, sizes), out_shape=(pltpu.VM...]
where the time goes in v2:
time: 28.8 us; the launch traced here: 28.7 us
  Pallas kernels  28 us (97%)
  between operations  0.64 us (2%)
    pallas_call x1, Pallas kernels, shards(): pl.pallas_call(functools.partial(step_kernel, sizes), out_shape=(pltpu.VM...  26.8 us
    pallas_call x1, Pallas kernels, shards(): pl.pallas_call(functools.partial(store_kernel, rows), out_shape=(jax.Shap...  1.2 us

profile of v2, /device:TPU:24, one launch (start us, length us, event | category | flops | bytes accessed | tf_op | source)
XLA Modules:
  0.0 28.7 jit_solution(10029792225041581966)
XLA Ops:
  0.6 26.8 %shard_map.76 = (f32[1152,128]{1,0:T(8,128)S(1)}, f32[1152,128]{1,0:T(8,128)S(1)}, f32[768,128]{1,0:T(8,128)S(1)}, f32[512,128]{1,0:T(8,128)S(1)}) custom-call(f32[1152,128]{1,0:T(8,128)} %bitcast.6, f32[1152,128]{1,0:T(8,128)} %bitcast.7, f32[768,128]{1,0:T(8,128)} %bitcast.8, s32[32,128]{1,0:T(8,128)} %mat_in.1, f32[32,128]{1,0:T(8,128)} %drv_in.1), custom_call_target="tpu_custom_call" | custom-call | tf_op jit(solution)/shard_map/pallas_call | solution.py:555
  27.5 1.2 %shard_map.77 = (f32[1152,128]{1,0:T(8,128)}, f32[1152,128]{1,0:T(8,128)}, f32[768,128]{1,0:T(8,128)}) custom-call(f32[1152,128]{1,0:T(8,128)S(1)} %get-tuple-element.10.e, f32[1152,128]{1,0:T(8,128)S(1)} %get-tuple-element.11.h, f32[768,128]{1,0:T(8,128)S(1)} %get-tuple-element.12.m, f32[512,128]{1,0:T(8,128)S(1)} %get-tuple-element.13.back_got), custom_call_target="tpu_custom_call" | custom-call | tf_op jit(solution)/shard_map/pallas_call | solution.py:593

commit v3 on v2

--- a/solution.py
+++ b/solution.py
@@ -88,8 +88,6 @@
         pltpu.make_async_copy(src, dst, load_sem.at[i])
         for i, (src, dst) in enumerate(((h_in, h), (e_in, e), (mat_in, mat), (drv_in, drv)))
     ]
-    for load in m_loads[0] + m_loads[1] + loads:
-        load.start()
 
     barrier = pltpu.get_barrier_semaphore()
 
@@ -106,6 +104,9 @@
     @pl.when(has_prev)
     def _():
         greet(to_a_prev)
+
+    for load in m_loads[0] + m_loads[1] + loads:
+        load.start()
 
     lane = lax.broadcasted_iota(jnp.int32, (TILE, LANES), 1)
     wide = lax.broadcasted_iota(jnp.int32, (rows, LANES), 1)
@@ -428,6 +429,35 @@
                     part(back, half, i), part(back_got, half, b), back_sem.at[half]
                 ).start()
 
+    def work(half, lo, hi):
+        for first in range(lo, hi, TILE):
+            spin(first, min(TILE, hi - first), 1, half)
+
+        def within(row):
+            return jnp.logical_and(row >= lo, row < hi)
+
+        for offset in everyone:
+            row = member(offset)
+
+            @pl.when(within(row))
+            def _():
+                pltpu.make_async_remote_copy(
+                    src_ref=part(back, half, row),
+                    dst_ref=part(back_got, half, b),
+                    send_sem=send_sem.at[2 + half],
+                    recv_sem=back_sem.at[half],
+                    device_id=peer(row),
+                    device_id_type=MESH,
+                ).start()
+
+        @pl.when(within(b))
+        def _():
+            pltpu.make_async_copy(
+                part(back, half, b), part(back_got, half, b), back_sem.at[half]
+            ).start()
+
+    everyone = [(step, turn) for step in far for turn in range(SEATS)] + mates
+
     def inner(half, lo, hi):
         for first in range(lo, hi, TILE):
             count = min(TILE, hi - first)
@@ -459,12 +489,13 @@
     inner(0, cuts[1], rows - 1)
     pass_low(1)
     outer(0, rows - 1)
+    early = rows // 2
     wait_wave(1, 1, rows - 2)
-    inner(1, 1, cuts[2])
+    work(1, 1, rows // 4)
     outer(1, 0)
-    inner(1, cuts[2], rows - 1)
+    work(1, rows // 4, early)
+    work(1, early, rows - 1)
     outer(1, rows - 1)
-
     for half in range(2):
         landed = back_got.at[pl.ds(half * group * 2 * HALF, group * 2 * HALF)]
         pltpu.make_async_copy(landed, landed, back_sem.at[half]).wait()

time: 28.8 us -> 28.8 us (level)
  no operation moved by 1% of the time
where the time goes in v3:
time: 28.8 us; the launch traced here: 28.7 us
  Pallas kernels  28 us (97%)
  between operations  0.64 us (2%)
    pallas_call x1, Pallas kernels, shards(): pl.pallas_call(functools.partial(step_kernel, sizes), out_shape=(pltpu.VM...  26.8 us
    pallas_call x1, Pallas kernels, shards(): pl.pallas_call(functools.partial(store_kernel, rows), out_shape=(jax.Shap...  1.2 us

profile of v3, /device:TPU:24, one launch (start us, length us, event | category | flops | bytes accessed | tf_op | source)
XLA Modules:
  0.0 28.7 jit_solution(734049049092525626)
XLA Ops:
  0.6 26.8 %shard_map.76 = (f32[1152,128]{1,0:T(8,128)S(1)}, f32[1152,128]{1,0:T(8,128)S(1)}, f32[768,128]{1,0:T(8,128)S(1)}, f32[512,128]{1,0:T(8,128)S(1)}) custom-call(f32[1152,128]{1,0:T(8,128)} %bitcast.6, f32[1152,128]{1,0:T(8,128)} %bitcast.7, f32[768,128]{1,0:T(8,128)} %bitcast.8, s32[32,128]{1,0:T(8,128)} %mat_in.1, f32[32,128]{1,0:T(8,128)} %drv_in.1), custom_call_target="tpu_custom_call" | custom-call | tf_op jit(solution)/shard_map/pallas_call | solution.py:586
  27.5 1.2 %shard_map.77 = (f32[1152,128]{1,0:T(8,128)}, f32[1152,128]{1,0:T(8,128)}, f32[768,128]{1,0:T(8,128)}) custom-call(f32[1152,128]{1,0:T(8,128)S(1)} %get-tuple-element.10.e, f32[1152,128]{1,0:T(8,128)S(1)} %get-tuple-element.11.h, f32[768,128]{1,0:T(8,128)S(1)} %get-tuple-element.12.m, f32[512,128]{1,0:T(8,128)S(1)} %get-tuple-element.13.back_got), custom_call_target="tpu_custom_call" | custom-call | tf_op jit(solution)/shard_map/pallas_call | solution.py:624

commit v4 on v3

--- a/solution.py
+++ b/solution.py
@@ -192,14 +192,14 @@
         def _():
             copy.start()
 
+    pending = []
+
     def land(copy, sends, receives):
         @pl.when(receives)
         def _():
             copy.wait_recv()
 
-        @pl.when(sends)
-        def _():
-            copy.wait_send()
+        pending.append((copy, sends))
 
     def block(ref, index, size):
         return ref.at[pl.ds(pl.multiple_of(index * PITCH, PITCH), size)]
@@ -259,7 +259,7 @@
     upper_step = step_dt / (eps * (1.0 + sigma))
 
     land(hx, has_next, has_prev)
-    hy.wait()
+    hy.wait_recv()
     left = jnp.where(b == 0, 0.0, hy_got[...])
 
     def below_x(v, n, z):
@@ -331,7 +331,7 @@
     pass_low(0)
 
     land(ex, has_prev, has_next)
-    ey.wait()
+    ey.wait_recv()
     right = jnp.where(b == group - 1, 0.0, ey_got[...])
 
     def above_x(v, n, z):
@@ -501,6 +501,14 @@
         pltpu.make_async_copy(landed, landed, back_sem.at[half]).wait()
         if half == 0:
             turn_magnet(m, back_got, group, half)
+
+    hy.wait_send()
+    ey.wait_send()
+    for copy, sends in pending:
+
+        @pl.when(sends)
+        def _():
+            copy.wait_send()
 
     for sem, size in enumerate((3 * CUT + 1, 3 * (FZ - CUT), 2 * HALF, 2 * HALF)):
         sent = chunk_a.at[pl.ds(0, (group - 1) * size)]

time: 28.8 us -> 28.8 us (level)
  no operation moved by 1% of the time
where the time goes in v4:
time: 28.8 us; the launch traced here: 28.7 us
  Pallas kernels  28 us (97%)
  between operations  0.64 us (2%)
    pallas_call x1, Pallas kernels, shards(): pl.pallas_call(functools.partial(step_kernel, sizes), out_shape=(pltpu.VM...  26.8 us
    pallas_call x1, Pallas kernels, shards(): pl.pallas_call(functools.partial(store_kernel, rows), out_shape=(jax.Shap...  1.2 us

profile of v4, /device:TPU:24, one launch (start us, length us, event | category | flops | bytes accessed | tf_op | source)
XLA Modules:
  0.0 28.7 jit_solution(12262975294936575566)
XLA Ops:
  0.6 26.8 %shard_map.76 = (f32[1152,128]{1,0:T(8,128)S(1)}, f32[1152,128]{1,0:T(8,128)S(1)}, f32[768,128]{1,0:T(8,128)S(1)}, f32[512,128]{1,0:T(8,128)S(1)}) custom-call(f32[1152,128]{1,0:T(8,128)} %bitcast.6, f32[1152,128]{1,0:T(8,128)} %bitcast.7, f32[768,128]{1,0:T(8,128)} %bitcast.8, s32[32,128]{1,0:T(8,128)} %mat_in.1, f32[32,128]{1,0:T(8,128)} %drv_in.1), custom_call_target="tpu_custom_call" | custom-call | tf_op jit(solution)/shard_map/pallas_call | solution.py:594
  27.5 1.2 %shard_map.77 = (f32[1152,128]{1,0:T(8,128)}, f32[1152,128]{1,0:T(8,128)}, f32[768,128]{1,0:T(8,128)}) custom-call(f32[1152,128]{1,0:T(8,128)S(1)} %get-tuple-element.10.e, f32[1152,128]{1,0:T(8,128)S(1)} %get-tuple-element.11.h, f32[768,128]{1,0:T(8,128)S(1)} %get-tuple-element.12.m, f32[512,128]{1,0:T(8,128)S(1)} %get-tuple-element.13.back_got), custom_call_target="tpu_custom_call" | custom-call | tf_op jit(solution)/shard_map/pallas_call | solution.py:632
